TPU v7x, 32 devices: a whole 2x2x4 slice. The times are simulated.
32 devices in a mesh: col: 4 (over z), row: 8 (over y, x, core).
Axes of the slice: x: 2, y: 2, z: 4, core: 2. Of those that a mesh axis runs over, the one named last changes fastest.
Arguments:
- factor: float32 [8192, 2048], P('row', 'col'), may hold values from -100 to 100
- support: int32 [16, 64], P(None, 'row'), may hold values from 0 to 1, as said below
- plan: int32 [2, 16], replicated, may hold values from 0 to 15, as said below
Outputs:
- rotated_factor: float32 [8192, 2048], P('row', 'col')
Inputs may be any that keep to these rules, and one draw needn't show every extreme that they name: Every column block has at least one row block in its support. `plan`: each row is a permutation; cut each round's row into groups of 4 consecutive positions (group g on index g of col); the 4 blocks of any group sit in 4 different groups of the previous round's row, where the order before round 0 is 0, 1, ..., 15.
All inputs are finite; a program needn't handle non-finite values.
Results may differ from a plain program's by a relative error of at most 0.0003.
Values sent between devices are 32-bit elements; how exact they have to be, the bound alone decides.
A program may use at most 128 MiB of HBM per device.

v0:
```python
import jax
import jax.numpy as jnp
from jax import lax
from jax.sharding import PartitionSpec as P

W = 128
RB = 128
ROUNDS = 2
precise = lax.Precision.HIGHEST
damping = 0.01


def skew_terms(gram_rows, diag_rows, diag_cols):
    spread = diag_rows[:, :, None] - diag_cols[:, None, :]
    joined = diag_rows[:, :, None] + diag_cols[:, None, :]
    return (
        gram_rows * spread / (spread * spread + gram_rows * gram_rows + damping * joined * joined)
    )


def cayley(skew_matrix):
    size_here = skew_matrix.shape[0]
    identity = jnp.eye(size_here, dtype=jnp.float32)
    halved = 0.5 * skew_matrix
    minus_half = identity - halved
    numerator = jnp.dot(minus_half, minus_half, precision=precise)
    definite = identity + jnp.dot(halved.T, halved, precision=precise)
    lower_factor = jnp.linalg.cholesky(definite)
    return jax.scipy.linalg.cho_solve((lower_factor, True), numerator)


def local_gram(left_cols, right_cols):
    return jnp.einsum("rpi,rpj->pij", left_cols, right_cols, precision=precise)


def on_device(factor, support, plan):
    rows_here = factor.shape[0]
    slot_count = factor.shape[1] // W
    group_count = lax.axis_size("col")
    col_place = lax.axis_index("col")
    pair_count = slot_count // 2
    own_support = lax.dynamic_slice_in_dim(support, col_place * slot_count, slot_count, 0)
    row_mask = jnp.repeat(own_support.T, RB, axis=0).astype(jnp.float32)
    current = factor.reshape(rows_here, slot_count, W) * row_mask[:, :, None]
    previous = jnp.arange(slot_count * group_count, dtype=jnp.int32)
    my_slots = col_place * slot_count + jnp.arange(slot_count, dtype=jnp.int32)
    group_ids = jnp.arange(group_count, dtype=jnp.int32)
    for round_index in range(ROUNDS):
        order_now = plan[round_index]
        located = jnp.argsort(previous)[order_now]
        wanted = located[my_slots]
        new_place = jnp.argsort(order_now)[previous[my_slots]]
        send_pick = (new_place[None, :] // slot_count == group_ids[:, None]).astype(jnp.float32)
        outgoing = jnp.einsum("dt,rtw->rdw", send_pick, current, precision=precise)
        incoming = lax.all_to_all(outgoing, "col", split_axis=1, concat_axis=1, tiled=True)
        take_pick = (wanted[:, None] // slot_count == group_ids[None, :]).astype(jnp.float32)
        arranged = jnp.einsum("sd,rdw->rsw", take_pick, incoming, precision=precise)
        paired = arranged.reshape(rows_here, pair_count, 2 * W)
        gram_matrix = lax.psum(local_gram(paired, paired), "row")
        diagonal_terms = jnp.diagonal(gram_matrix, axis1=1, axis2=2)
        skew_matrix = skew_terms(gram_matrix, diagonal_terms, diagonal_terms)
        rotations = jax.vmap(cayley)(skew_matrix)
        rotated = jnp.einsum("rpi,pij->rpj", paired, rotations, precision=precise)
        current = rotated.reshape(rows_here, slot_count, W)
        previous = order_now
    return current.reshape(rows_here, slot_count * W)


def solution(mesh):
    return jax.shard_map(
        on_device,
        mesh=mesh,
        in_specs=(P("row", "col"), P(None, "row"), P()),
        out_specs=P("row", "col"),
        check_vma=False,
    )
```

profile of v0, /device:TPU:0, one launch (start us, length us, event | category | flops | bytes accessed | tf_op | source)
XLA Modules:
  0.0 565.6 jit_solution(1841204664896612224)
XLA Ops:
  14.5 4.0 fusion.14
  20.0 6.4 %all-to-all-start = ((f32[1024,4,128]{2,0,1:T(8,128)}), f32[1024,4,128]{2,0,1:T(8,128)S(1)}, u32[]{:S(2)}, u32[]{:S(2)}) async-start(f32[1024,4,128]{2,0,1:T(8,128)} %copy.118), calls=%async_computation | async-start | bytes 4194304 | tf_op jit(solution)/shard_map/all_to_all | solution.py:55
  29.1 45.5 %all-to-all-done = f32[1024,4,128]{2,0,1:T(8,128)S(1)} async-done(((f32[1024,4,128]{2,0,1:T(8,128)}), f32[1024,4,128]{2,0,1:T(8,128)S(1)}, u32[]{:S(2)}, u32[]{:S(2)}) %all-to-all-start) | async-done | bytes 2097184 | tf_op jit(solution)/shard_map/all_to_all | solution.py:55
  74.6 4.6 fusion.17
  79.2 3.4 reshape.294
  82.6 4.3 fusion.12
  87.0 53.7 %all-reduce.4.cloned.1.call-done = f32[2,256,256]{1,2,0:T(8,128)} async-done(((f32[2,256,256]{1,2,0:T(8,128)}), f32[2,256,256]{1,2,0:T(8,128)}) %all-reduce.4.cloned.1.call-update) | async-done | bytes 524304 | tf_op jit(solution)/shard_map/psum | solution.py:59
  140.7 17.2 %copy.123 = f32[2,256,256]{0,2,1:T(8,128)} copy(f32[2,256,256]{1,2,0:T(8,128)} %all-reduce.4.cloned.1.call-done) | data formatting | bytes 1048576 | tf_op jit(solution)/shard_map/psum | solution.py:59
  157.9 2.3 gather_fusion.4
  162.5 23.5 %custom-call.23 = f32[2,128,128]{2,1,0:T(8,128)S(1)} custom-call(f32[2,128,128]{2,1,0:T(8,128)S(1)} %cholesky.198), custom_call_target="Cholesky" | custom-call | tf_op jit(solution)/shard_map/vmap(jit(cholesky))/cholesky | solution.py:28
  186.1 20.2 %custom-call.24 = f32[2,1,128,128]{2,3,1,0:T(8,128)S(1)} custom-call(f32[2,1,128,128]{3,2,1,0:T(8,128)S(1)} %select_bitcast_fusion.1), custom_call_target="InvertDiagBlocksLowerTriangular" | custom-call | tf_op jit(solution)/shard_map/vmap(jit(cholesky))/cholesky | solution.py:28
  208.8 23.5 %custom-call.25 = f32[2,128,128]{2,1,0:T(8,128)S(1)} custom-call(f32[2,128,128]{2,1,0:T(8,128)S(1)} %convolution_subtract_fusion.5), custom_call_target="Cholesky" | custom-call | tf_op jit(solution)/shard_map/vmap(jit(cholesky))/cholesky | solution.py:28
  232.8 4.1 while.4
  236.9 39.5 %custom-call.26 = f32[2,2,128,128]{2,3,1,0:T(8,128)S(1)} custom-call(f32[2,2,128,128]{3,2,1,0:T(8,128)S(1)} %bitcast.143), custom_call_target="InvertDiagBlocksLowerTriangular" | custom-call | tf_op jit(solution)/shard_map/vmap(jit(_cho_solve))/triangular_solve | solution.py:29
  276.4 2.7 fusion.42
  281.6 4.9 fusion.10
  292.1 4.5 all-to-all-start.1
  298.0 46.2 %all-to-all-done.1 = f32[1024,4,128]{2,0,1:T(8,128)} async-done(((f32[1024,4,128]{2,0,1:T(8,128)}), f32[1024,4,128]{2,0,1:T(8,128)}, u32[]{:S(2)}, u32[]{:S(2)}) %all-to-all-start.1) | async-done | bytes 2097184 | tf_op jit(solution)/shard_map/all_to_all | solution.py:55
  344.1 6.1 %fusion.20 = f32[1024,4,128]{2,1,0:T(4,128)} fusion(f32[1024,4,128]{2,0,1:T(8,128)} %all-to-all-done.1, s32[4]{0:T(128)S(1)} %and_select_fusion), kind=kOutput, calls=%fused_computation.30 | convolution fusion | flops 25165840 | bytes 4194320 | tf_op jit(solution)/shard_map/sd,rdw->rsw/dot_general | solution.py:57
  350.3 3.3 reshape.296
  353.6 4.3 fusion.8
  357.9 52.2 %all-reduce.6.cloned.1.call-done = f32[2,256,256]{1,2,0:T(8,128)} async-done(((f32[2,256,256]{1,2,0:T(8,128)}), f32[2,256,256]{1,2,0:T(8,128)}) %all-reduce.6.cloned.1.call-update) | async-done | bytes 524304 | tf_op jit(solution)/shard_map/psum | solution.py:59
  410.1 17.2 %copy.145 = f32[2,256,256]{0,2,1:T(8,128)} copy(f32[2,256,256]{1,2,0:T(8,128)} %all-reduce.6.cloned.1.call-done) | data formatting | bytes 1048576 | tf_op jit(solution)/shard_map/psum | solution.py:59
  427.3 2.3 gather_fusion.9
  432.0 23.5 %custom-call.27 = f32[2,128,128]{2,1,0:T(8,128)S(1)} custom-call(f32[2,128,128]{2,1,0:T(8,128)S(1)} %cholesky.201), custom_call_target="Cholesky" | custom-call | tf_op jit(solution)/shard_map/vmap(jit(cholesky))/cholesky | solution.py:28
  455.5 20.1 %custom-call.28 = f32[2,1,128,128]{2,3,1,0:T(8,128)S(1)} custom-call(f32[2,1,128,128]{3,2,1,0:T(8,128)S(1)} %select_bitcast_fusion), custom_call_target="InvertDiagBlocksLowerTriangular" | custom-call | tf_op jit(solution)/shard_map/vmap(jit(cholesky))/cholesky | solution.py:28
  478.1 23.5 %custom-call.29 = f32[2,128,128]{2,1,0:T(8,128)S(1)} custom-call(f32[2,128,128]{2,1,0:T(8,128)S(1)} %convolution_subtract_fusion.4), custom_call_target="Cholesky" | custom-call | tf_op jit(solution)/shard_map/vmap(jit(cholesky))/cholesky | solution.py:28
  502.0 4.1 while.5
  506.2 39.5 %custom-call.30 = f32[2,2,128,128]{2,3,1,0:T(8,128)S(1)} custom-call(f32[2,2,128,128]{3,2,1,0:T(8,128)S(1)} %bitcast.142), custom_call_target="InvertDiagBlocksLowerTriangular" | custom-call | tf_op jit(solution)/shard_map/vmap(jit(_cho_solve))/triangular_solve | solution.py:29
  545.7 2.7 fusion.40
  550.8 4.9 fusion.6
  555.7 2.9 copy.161
  (111 shorter events, 42.7 us)
Async XLA Ops:
  9.9 4.5 copy-start.4
  20.0 7.8 %copy-start.5 = (s32[2,16]{1,0:T(2,128)S(1)}, s32[2,16]{1,0:T(2,128)}, u32[]{:S(2)}) copy-start(s32[2,16]{1,0:T(2,128)} %param.8) | copy-start | bytes 388
  20.0 54.6 %all-to-all-start = ((f32[1024,4,128]{2,0,1:T(8,128)}), f32[1024,4,128]{2,0,1:T(8,128)S(1)}, u32[]{:S(2)}, u32[]{:S(2)}) async-start(f32[1024,4,128]{2,0,1:T(8,128)} %copy.118), calls=%async_computation | async-start | bytes 4194304 | tf_op jit(solution)/shard_map/all_to_all | solution.py:55
  26.4 114.3 %all-reduce.4.cloned.1.call-start = ((), (), s32[]{:S(2)}) async-start(), calls=%async_computation.2 | async-start | bytes 1048576 | tf_op jit(solution)/shard_map/psum | solution.py:59
  140.7 19.6 %copy-start.3 = (f32[2,256,256]{1,2,0:T(8,128)S(1)}, f32[2,256,256]{1,2,0:T(8,128)}, u32[]{:S(2)}) copy-start(f32[2,256,256]{1,2,0:T(8,128)} %all-reduce.4.cloned.1.call-done) | copy-start | bytes 1572868
  161.7 0.8 copy-start.1
  292.1 52.0 %all-to-all-start.1 = ((f32[1024,4,128]{2,0,1:T(8,128)}), f32[1024,4,128]{2,0,1:T(8,128)}, u32[]{:S(2)}, u32[]{:S(2)}) async-start(f32[1024,4,128]{2,0,1:T(8,128)} %copy.140), calls=%async_computation.1 | async-start | bytes 4194304 | tf_op jit(solution)/shard_map/all_to_all | solution.py:55
  296.7 113.5 %all-reduce.6.cloned.1.call-start = ((), (), s32[]{:S(2)}) async-start(), calls=%async_computation.3 | async-start | bytes 1048576 | tf_op jit(solution)/shard_map/psum | solution.py:59
  410.1 19.6 %copy-start.2 = (f32[2,256,256]{1,2,0:T(8,128)S(1)}, f32[2,256,256]{1,2,0:T(8,128)}, u32[]{:S(2)}) copy-start(f32[2,256,256]{1,2,0:T(8,128)} %all-reduce.6.cloned.1.call-done) | copy-start | bytes 1572868
  431.2 0.8 copy-start
Sparse Core Ops, SparseCore 0:
  87.0 53.6 all-reduce.3
  358.1 52.0 all-reduce.5
where the time goes:
time: 572 us; the launch traced here: 566 us
  other arithmetic  218 us (38%)
  waiting for transfers between devices  198 us (35%)
  local copies, waits for them, and re-layouts  72 us (13%)
  matrix products  52.7 us (9%)
  between operations  14.1 us (2%)
  starting transfers between devices  11 us (2%)
    another operation x18, other arithmetic, cayley(): lower_factor = jnp.linalg.cholesky(definite)  135 us
    psum x2, waiting for transfers between devices, on_device(): gram_matrix = lax.psum(local_gram(paired, paired), 'row')  106 us
    all_to_all x2, waiting for transfers between devices, on_device(): lax.all_to_all(outgoing, 'col', split_axis=1, concat_axis=1, tiled=True)  91.7 us
    another operation x6, other arithmetic, cayley(): return jax.scipy.linalg.cho_solve((lower_factor, True), numerator)  79.3 us
    psum x2, local copies, waits for them, and re-layouts, on_device(): gram_matrix = lax.psum(local_gram(paired, paired), 'row')  34.4 us
  transfers between devices with their start and end apart: 4, of which 4 were waited for; matrix products, arithmetic and copies ran while one was open for 1% of the time, Pallas kernels for 0%

commit v1 on v0

--- a/solution.py
+++ b/solution.py
@@ -2,12 +2,17 @@
 import jax.numpy as jnp
 from jax import lax
 from jax.sharding import PartitionSpec as P
+from jax.lax import all_gather
 
 W = 128
 RB = 128
 ROUNDS = 2
 precise = lax.Precision.HIGHEST
 damping = 0.01
+
+
+def pair_targets(raw):
+    return jnp.sum(all_gather(raw, "row"), axis=0)
 
 
 def skew_terms(gram_rows, diag_rows, diag_cols):
@@ -56,7 +61,7 @@
         take_pick = (wanted[:, None] // slot_count == group_ids[None, :]).astype(jnp.float32)
         arranged = jnp.einsum("sd,rdw->rsw", take_pick, incoming, precision=precise)
         paired = arranged.reshape(rows_here, pair_count, 2 * W)
-        gram_matrix = lax.psum(local_gram(paired, paired), "row")
+        gram_matrix = pair_targets(local_gram(paired, paired))
         diagonal_terms = jnp.diagonal(gram_matrix, axis1=1, axis2=2)
         skew_matrix = skew_terms(gram_matrix, diagonal_terms, diagonal_terms)
         rotations = jax.vmap(cayley)(skew_matrix)

time: 572 us -> 542 us (0.948)
  waiting for transfers between devices: 198 us -> 164 us
    psum x2 -> x0, waiting for transfers between devices: 106 us -> none  [on_device(): gram_matrix = lax.psum(local_gram(paired, paired), 'row')]
    all_gather x0 -> x2, waiting for transfers between devices: none -> 70.9 us  [pair_targets(): return jnp.sum(all_gather(raw, 'row'), axis=0)]
    psum x2 -> x0, local copies, waits for them, and re-layouts: 34.4 us -> none  [on_device(): gram_matrix = lax.psum(local_gram(paired, paired), 'row')]
    reduce_sum x0 -> x4, local copies, waits for them, and re-layouts: none -> 33.3 us  [pair_targets(): return jnp.sum(all_gather(raw, 'row'), axis=0)]
where the time goes in v1:
time: 542 us; the launch traced here: 537 us
  other arithmetic  223 us (41%)
  waiting for transfers between devices  164 us (30%)
  local copies, waits for them, and re-layouts  70.6 us (13%)
  matrix products  54.1 us (10%)
  between operations  14.1 us (3%)
  starting transfers between devices  11.2 us (2%)
    another operation x18, other arithmetic, cayley(): lower_factor = jnp.linalg.cholesky(definite)  135 us
    all_to_all x2, waiting for transfers between devices, on_device(): lax.all_to_all(outgoing, 'col', split_axis=1, concat_axis=1, tiled=True)  92.6 us
    another operation x6, other arithmetic, cayley(): return jax.scipy.linalg.cho_solve((lower_factor, True), numerator)  79.3 us
    all_gather x2, waiting for transfers between devices, pair_targets(): return jnp.sum(all_gather(raw, 'row'), axis=0)  70.9 us
    reduce_sum x4, local copies, waits for them, and re-layouts, pair_targets(): return jnp.sum(all_gather(raw, 'row'), axis=0)  33.3 us
    all_to_all x2, starting transfers between devices, on_device(): lax.all_to_all(outgoing, 'col', split_axis=1, concat_axis=1, tiled=True)  11 us
  transfers between devices with their start and end apart: 4, of which 4 were waited for; matrix products, arithmetic and copies ran while one was open for 1% of the time, Pallas kernels for 0%

profile of v1, /device:TPU:0, one launch (start us, length us, event | category | flops | bytes accessed | tf_op | source)
XLA Modules:
  0.0 536.9 jit_solution(11085884596073870667)
XLA Ops:
  14.5 4.0 fusion.14
  20.0 6.5 %all-to-all-start = ((f32[1024,4,128]{2,0,1:T(8,128)}), f32[1024,4,128]{2,0,1:T(8,128)S(1)}, u32[]{:S(2)}, u32[]{:S(2)}) async-start(f32[1024,4,128]{2,0,1:T(8,128)} %copy.118), calls=%async_computation | async-start | bytes 4194304 | tf_op jit(solution)/shard_map/all_to_all | solution.py:60
  29.1 45.6 %all-to-all-done = f32[1024,4,128]{2,0,1:T(8,128)S(1)} async-done(((f32[1024,4,128]{2,0,1:T(8,128)}), f32[1024,4,128]{2,0,1:T(8,128)S(1)}, u32[]{:S(2)}, u32[]{:S(2)}) %all-to-all-start) | async-done | bytes 2097184 | tf_op jit(solution)/shard_map/all_to_all | solution.py:60
  74.6 4.6 fusion.17
  79.2 3.4 reshape.294
  82.6 4.3 fusion.12
  87.1 35.9 %all-gather.5.cloned.1.call-done = f32[16,256,256]{2,1,0:T(8,128)} async-done(((f32[2,256,256]{2,1,0:T(8,128)}), f32[16,256,256]{2,1,0:T(8,128)}) %all-gather.5.cloned.1.call-update) | async-done | bytes 4194320 | tf_op jit(solution)/shard_map/all_gather | solution.py:15
  122.9 2.5 reduce_sum.18
  125.5 16.5 %copy.122 = f32[2,256,256]{0,2,1:T(8,128)} copy(f32[2,256,256]{2,1,0:T(8,128)S(1)} %reduce_sum.18) | data formatting | bytes 1048576 | tf_op jit(solution)/shard_map/reduce_sum | solution.py:15
  142.1 2.3 gather_fusion.4
  149.0 24.0 %custom-call.23 = f32[2,128,128]{2,1,0:T(8,128)S(1)} custom-call(f32[2,128,128]{2,1,0:T(8,128)S(1)} %cholesky.198), custom_call_target="Cholesky" | custom-call | tf_op jit(solution)/shard_map/vmap(jit(cholesky))/cholesky | solution.py:33
  173.1 19.7 %custom-call.24 = f32[2,1,128,128]{2,3,1,0:T(8,128)S(1)} custom-call(f32[2,1,128,128]{3,2,1,0:T(8,128)S(1)} %select_bitcast_fusion.1), custom_call_target="InvertDiagBlocksLowerTriangular" | custom-call | tf_op jit(solution)/shard_map/vmap(jit(cholesky))/cholesky | solution.py:33
  195.3 23.5 %custom-call.25 = f32[2,128,128]{2,1,0:T(8,128)S(1)} custom-call(f32[2,128,128]{2,1,0:T(8,128)S(1)} %convolution_subtract_fusion.5), custom_call_target="Cholesky" | custom-call | tf_op jit(solution)/shard_map/vmap(jit(cholesky))/cholesky | solution.py:33
  219.3 4.1 while.4
  223.4 39.5 %custom-call.26 = f32[2,2,128,128]{2,3,1,0:T(8,128)S(1)} custom-call(f32[2,2,128,128]{3,2,1,0:T(8,128)S(1)} %bitcast.147), custom_call_target="InvertDiagBlocksLowerTriangular" | custom-call | tf_op jit(solution)/shard_map/vmap(jit(_cho_solve))/triangular_solve | solution.py:34
  267.2 4.8 fusion.10
  277.8 4.6 all-to-all-start.1
  283.9 47.1 %all-to-all-done.1 = f32[1024,4,128]{2,0,1:T(8,128)S(1)} async-done(((f32[1024,4,128]{2,0,1:T(8,128)}), f32[1024,4,128]{2,0,1:T(8,128)S(1)}, u32[]{:S(2)}, u32[]{:S(2)}) %all-to-all-start.1) | async-done | bytes 2097184 | tf_op jit(solution)/shard_map/all_to_all | solution.py:60
  331.0 4.6 fusion.20
  335.5 3.1 reshape.296
  338.7 4.3 fusion.8
  343.0 35.0 %all-gather.7.cloned.1.call-done = f32[16,256,256]{2,1,0:T(8,128)} async-done(((f32[2,256,256]{2,1,0:T(8,128)}), f32[16,256,256]{2,1,0:T(8,128)}) %all-gather.7.cloned.1.call-update) | async-done | bytes 4194320 | tf_op jit(solution)/shard_map/all_gather | solution.py:15
  378.0 2.5 reduce_sum.19
  380.6 16.5 %copy.146 = f32[2,256,256]{0,2,1:T(8,128)} copy(f32[2,256,256]{2,1,0:T(8,128)S(1)} %reduce_sum.19) | data formatting | bytes 1048576 | tf_op jit(solution)/shard_map/reduce_sum | solution.py:15
  397.3 2.3 gather_fusion.9
  404.1 23.9 %custom-call.27 = f32[2,128,128]{2,1,0:T(8,128)S(1)} custom-call(f32[2,128,128]{2,1,0:T(8,128)S(1)} %cholesky.201), custom_call_target="Cholesky" | custom-call | tf_op jit(solution)/shard_map/vmap(jit(cholesky))/cholesky | solution.py:33
  428.1 19.7 %custom-call.28 = f32[2,1,128,128]{2,3,1,0:T(8,128)S(1)} custom-call(f32[2,1,128,128]{3,2,1,0:T(8,128)S(1)} %select_bitcast_fusion), custom_call_target="InvertDiagBlocksLowerTriangular" | custom-call | tf_op jit(solution)/shard_map/vmap(jit(cholesky))/cholesky | solution.py:33
  450.3 23.5 %custom-call.29 = f32[2,128,128]{2,1,0:T(8,128)S(1)} custom-call(f32[2,128,128]{2,1,0:T(8,128)S(1)} %convolution_subtract_fusion.4), custom_call_target="Cholesky" | custom-call | tf_op jit(solution)/shard_map/vmap(jit(cholesky))/cholesky | solution.py:33
  474.2 4.1 while.5
  478.3 39.5 %custom-call.30 = f32[2,2,128,128]{2,3,1,0:T(8,128)S(1)} custom-call(f32[2,2,128,128]{3,2,1,0:T(8,128)S(1)} %bitcast.146), custom_call_target="InvertDiagBlocksLowerTriangular" | custom-call | tf_op jit(solution)/shard_map/vmap(jit(_cho_solve))/triangular_solve | solution.py:34
  522.1 4.9 fusion.6
  527.0 2.9 copy.165
  (111 shorter events, 51.5 us)
Async XLA Ops:
  9.9 4.5 copy-start.2
  20.0 7.8 %copy-start.3 = (s32[2,16]{1,0:T(2,128)S(1)}, s32[2,16]{1,0:T(2,128)}, u32[]{:S(2)}) copy-start(s32[2,16]{1,0:T(2,128)} %param.8) | copy-start | bytes 388
  20.0 54.6 %all-to-all-start = ((f32[1024,4,128]{2,0,1:T(8,128)}), f32[1024,4,128]{2,0,1:T(8,128)S(1)}, u32[]{:S(2)}, u32[]{:S(2)}) async-start(f32[1024,4,128]{2,0,1:T(8,128)} %copy.118), calls=%async_computation | async-start | bytes 4194304 | tf_op jit(solution)/shard_map/all_to_all | solution.py:60
  26.4 96.5 %all-gather.5.cloned.1.call-start = ((), (), s32[]{:S(2)}) async-start(), calls=%async_computation.2 | async-start | bytes 4718592 | tf_op jit(solution)/shard_map/all_gather | solution.py:15
  148.2 0.8 copy-start.1
  277.8 53.2 %all-to-all-start.1 = ((f32[1024,4,128]{2,0,1:T(8,128)}), f32[1024,4,128]{2,0,1:T(8,128)S(1)}, u32[]{:S(2)}, u32[]{:S(2)}) async-start(f32[1024,4,128]{2,0,1:T(8,128)} %copy.142), calls=%async_computation.1 | async-start | bytes 4194304 | tf_op jit(solution)/shard_map/all_to_all | solution.py:60
  282.4 95.7 %all-gather.7.cloned.1.call-start = ((), (), s32[]{:S(2)}) async-start(), calls=%async_computation.3 | async-start | bytes 4718592 | tf_op jit(solution)/shard_map/all_gather | solution.py:15
  403.3 0.8 copy-start
Sparse Core Ops, SparseCore 0:
  87.1 35.8 all-gather.4
  343.2 34.8 all-gather.6
